TPU v7x, 32 devices: a whole 2x2x4 slice. The times are simulated.
32 devices in a mesh: dp: 1, expert: 32 (over z, y, x, core).
Axes of the slice: x: 2, y: 2, z: 4, core: 2. Of those that a mesh axis runs over, the one named last changes fastest.
Arguments:
- tokens: bfloat16 [4096, 2048], P(('dp', 'expert')), may hold values from -6 to 6
- upstream: bfloat16 [4096, 2048], P(('dp', 'expert')), may hold values from -6 to 6
- w_up: bfloat16 [32, 2048, 768], P('expert'), may hold values from -0.125 to 0.125
- w_down: bfloat16 [32, 2048, 768], P('expert'), may hold values from -0.21875 to 0.21875
- routes: int32 [4096, 1], P(('dp', 'expert')), may hold values from 0 to 31; in each aligned block of 128 rows (0 to 127, 128 to 255, ...) at most 6 rows name the same one
- gate_share: int32 [4096, 1], P(('dp', 'expert')), may hold values from 1 to 256
Outputs:
- token_grad: bfloat16 [4096, 2048], P(('dp', 'expert'))
- gate_grad: bfloat16 [4096, 1], P(('dp', 'expert'))
- up_grad: float32 [32, 2048, 768], P('expert', 'dp')
- down_grad: float32 [32, 2048, 768], P('expert', 'dp')
Inputs may be any that keep to these rules, and one draw needn't show every extreme that they name: `routes`: within the 128 tokens of one device each expert is named by at most 6 rows, and by exactly 6 for some expert.
All inputs are finite; a program needn't handle non-finite values.
Results may differ from a plain program's by a relative error of at most 0.013.
Values may be sent and summed in bfloat16 or wider, within the bound.
A program may use at most 64 MiB of HBM per device.

v0:
```python
import jax
import jax.numpy as jnp
from jax import lax
from jax.sharding import PartitionSpec as P

EXP_DEV = 1
GATE_DEN = 256
TOK_DEV = 128


def expert_rows(got_tokens, got_upstream, got_gates, up_weight, down_weight):
    pre_act = jnp.einsum("pnd,df->pnf", got_tokens, up_weight, preferred_element_type=jnp.float32)
    hidden = jax.nn.silu(pre_act).astype(jnp.bfloat16)
    expert_out = jnp.einsum("pnf,df->pnd", hidden, down_weight, preferred_element_type=jnp.float32)
    gate_grad = jnp.sum(expert_out * got_upstream.astype(jnp.float32), axis=-1).astype(jnp.bfloat16)
    scaled = (got_gates.astype(jnp.float32)[..., None] * got_upstream.astype(jnp.float32)).astype(
        jnp.bfloat16
    )
    hidden_grad = jnp.einsum("pnd,df->pnf", scaled, down_weight, preferred_element_type=jnp.float32)
    sigmoid_a = jax.nn.sigmoid(pre_act)
    pre_grad = (hidden_grad * sigmoid_a * (1.0 + pre_act * (1.0 - sigmoid_a))).astype(jnp.bfloat16)
    row_grad = jnp.einsum(
        "pnf,df->pnd", pre_grad, up_weight, preferred_element_type=jnp.float32
    ).astype(jnp.bfloat16)
    return (row_grad, gate_grad, hidden, scaled, pre_grad)


def per_device(tokens, upstream, w_up, w_down, routes, gate_share):
    token_count, feature_count = tokens.shape
    top_count = routes.shape[1]
    peer_count = lax.axis_size("expert")
    expert_total = peer_count * EXP_DEV
    slot_count = (3 * TOK_DEV * top_count + 2 * expert_total - 1) // (2 * expert_total)
    up_weight = w_up[0]
    down_weight = w_down[0]
    flat_routes = routes.reshape(-1)
    row_count = flat_routes.shape[0]
    row_ids = jnp.arange(row_count, dtype=jnp.int32)
    same_expert = flat_routes[:, None] == flat_routes[None, :]
    earlier = row_ids[None, :] < row_ids[:, None]
    slot_rank = jnp.sum(same_expert & earlier, axis=1)
    slot_index = flat_routes * slot_count + slot_rank
    slot_owner = (
        jnp.full((peer_count * slot_count,), row_count, jnp.int32).at[slot_index].set(row_ids)
    )
    source_token = slot_owner // top_count
    send_tokens = jnp.take(tokens, source_token, axis=0, mode="fill", fill_value=0).reshape(
        peer_count, slot_count, feature_count
    )
    send_upstream = jnp.take(upstream, source_token, axis=0, mode="fill", fill_value=0).reshape(
        peer_count, slot_count, feature_count
    )
    gate_values = gate_share.reshape(-1).astype(jnp.float32) / GATE_DEN
    send_gates = (
        jnp.take(gate_values, slot_owner, axis=0, mode="fill", fill_value=0)
        .astype(jnp.bfloat16)
        .reshape(peer_count, slot_count)
    )
    got_tokens, got_upstream, got_gates = (
        lax.all_to_all(send_tokens, "expert", split_axis=0, concat_axis=0, tiled=True),
        lax.all_to_all(send_upstream, "expert", split_axis=0, concat_axis=0, tiled=True),
        lax.all_to_all(send_gates, "expert", split_axis=0, concat_axis=0, tiled=True),
    )
    row_grad, gate_grad, hidden, scaled, pre_grad = expert_rows(
        got_tokens, got_upstream, got_gates, up_weight, down_weight
    )
    back_rows, back_gates = (
        lax.all_to_all(row_grad, "expert", split_axis=0, concat_axis=0, tiled=True),
        lax.all_to_all(gate_grad, "expert", split_axis=0, concat_axis=0, tiled=True),
    )
    row_results = back_rows.reshape(-1, feature_count)[slot_index]
    token_grad = (
        row_results.astype(jnp.float32)
        .reshape(token_count, top_count, feature_count)
        .sum(axis=1)
        .astype(jnp.bfloat16)
    )
    gate_grad_out = back_gates.reshape(-1)[slot_index].reshape(token_count, top_count)
    flat_tokens = got_tokens.reshape(-1, feature_count)
    flat_scaled = scaled.reshape(-1, feature_count)
    flat_pre = pre_grad.reshape(-1, pre_grad.shape[-1])
    flat_hidden = hidden.reshape(-1, hidden.shape[-1])
    columns = flat_tokens
    up_grad = lax.psum_scatter(
        jnp.einsum("sc,sf->cf", columns, flat_pre, preferred_element_type=jnp.float32).astype(
            jnp.bfloat16
        ),
        "dp",
        scatter_dimension=0,
        tiled=True,
    ).astype(jnp.float32)
    columns = flat_scaled
    down_grad = lax.psum_scatter(
        jnp.einsum("sc,sf->cf", columns, flat_hidden, preferred_element_type=jnp.float32).astype(
            jnp.bfloat16
        ),
        "dp",
        scatter_dimension=0,
        tiled=True,
    ).astype(jnp.float32)
    return (token_grad, gate_grad_out, up_grad[None], down_grad[None])


def solution(mesh):
    return jax.shard_map(
        per_device,
        mesh=mesh,
        in_specs=(
            P(("dp", "expert"), None),
            P(("dp", "expert"), None),
            P("expert", None, None),
            P("expert", None, None),
            P(("dp", "expert"), None),
            P(("dp", "expert"), None),
        ),
        out_specs=(
            P(("dp", "expert"), None),
            P(("dp", "expert"), None),
            P("expert", "dp", None),
            P("expert", "dp", None),
        ),
        check_vma=False,
    )
```

profile of v0, /device:TPU:0, one launch (start us, length us, event | category | flops | bytes accessed | tf_op | source)
XLA Modules:
  0.0 140.6 jit_solution(5102218702544087126)
XLA Ops:
  0.6 0.0 copy-start
  0.6 0.8 multiply_bitcast_fusion
  1.5 1.0 convert_reduce_fusion
  2.4 0.7 fusion.34
  3.1 1.0 scatter_custom_fusion
  4.1 1.6 %gather_fusion = bf16[192]{0:T(256)(128)(2,1)S(1)} fusion(bf16[128]{0:T(256)(128)(2,1)S(1)} %multiply_bitcast_fusion, s32[1024]{0:T(1024)S(1)} %pad_clamp_fusion.1), kind=kCustom, calls=%fused_computation.2 | custom fusion | bytes 1536 | tf_op jit(solution)/shard_map/jit(_take)/gather | solution.py:55
  5.7 0.7 convert_element_type.88
  6.4 7.3 %all-to-all-start = ((bf16[32,1,6]{2,1,0:T(2,128)(2,1)}), bf16[32,1,6]{2,1,0:T(2,128)(2,1)S(1)}, u32[]{:S(2)}, u32[]{:S(2)}) async-start(bf16[32,1,6]{2,1,0:T(2,128)(2,1)} %convert_element_type.88), calls=%async_computation | async-start | bytes 32768 | tf_op jit(solution)/shard_map/all_to_all | solution.py:62
  13.7 3.9 %gather_fusion.4 = bf16[192,2048]{1,0:T(8,128)(2,1)} fusion(bf16[128,2048]{1,0:T(8,128)(2,1)} %param.8, s32[1024]{0:T(1024)S(1)} %pad_clamp_fusion.1), kind=kCustom, calls=%fused_computation.1.clone | custom fusion | bytes 1573632 | tf_op jit(solution)/shard_map/jit(_take)/gather | solution.py:47
  17.6 3.9 %gather_fusion.3 = bf16[192,2048]{1,0:T(8,128)(2,1)} fusion(bf16[128,2048]{1,0:T(8,128)(2,1)} %param.9, s32[1024]{0:T(1024)S(1)} %pad_clamp_fusion.1), kind=kCustom, calls=%fused_computation.clone | custom fusion | bytes 1573632 | tf_op jit(solution)/shard_map/jit(_take)/gather | solution.py:50
  21.5 2.7 %broadcast_select_fusion.1 = (bf16[192,2048]{1,0:T(8,128)(2,1)}, bf16[192,2048]{1,0:T(8,128)(2,1)}) fusion(bf16[192,2048]{1,0:T(8,128)(2,1)} %gather_fusion.3, pred[192]{0:T(512)(128)(4,1)S(1)} %get-tuple-element.6, bf16[192,2048]{1,0:T(8,128)(2,1)} %gather_fusion.4), kind=kLoop, calls=%fused_computation.27 | loop fusion | flops 786432 | bytes 3145920 | tf_op jit(solution)/shard_map/jit(_take)/select_n | solution.py:50
  24.2 2.2 %reshape.94 = bf16[32,6,2048]{2,1,0:T(8,128)(2,1)} reshape(bf16[192,2048]{1,0:T(8,128)(2,1)} %get-tuple-element.8) | data formatting | bytes 1572864 | tf_op jit(solution)/shard_map/reshape | solution.py:47
  26.4 0.0 all-to-all-done
  26.4 6.0 %all-to-all-start.2 = ((bf16[32,6,2048]{2,1,0:T(8,128)(2,1)}), bf16[32,6,2048]{2,1,0:T(8,128)(2,1)}, u32[]{:S(2)}, u32[]{:S(2)}) async-start(bf16[32,6,2048]{2,1,0:T(8,128)(2,1)} %reshape.94), calls=%async_computation.2 | async-start | bytes 2097152 | tf_op jit(solution)/shard_map/all_to_all | solution.py:60
  32.3 2.2 %reshape.93 = bf16[32,6,2048]{2,1,0:T(8,128)(2,1)} reshape(bf16[192,2048]{1,0:T(8,128)(2,1)} %get-tuple-element.7) | data formatting | bytes 1572864 | tf_op jit(solution)/shard_map/reshape | solution.py:50
  34.5 24.0 %all-to-all-done.2 = bf16[32,6,2048]{2,1,0:T(8,128)(2,1)} async-done(((bf16[32,6,2048]{2,1,0:T(8,128)(2,1)}), bf16[32,6,2048]{2,1,0:T(8,128)(2,1)}, u32[]{:S(2)}, u32[]{:S(2)}) %all-to-all-start.2) | async-done | bytes 786464 | tf_op jit(solution)/shard_map/all_to_all | solution.py:60
  58.6 3.7 %all-to-all-start.1 = ((bf16[32,6,2048]{2,1,0:T(8,128)(2,1)}), bf16[32,6,2048]{2,1,0:T(8,128)(2,1)}, u32[]{:S(2)}, u32[]{:S(2)}) async-start(bf16[32,6,2048]{2,1,0:T(8,128)(2,1)} %reshape.93), calls=%async_computation.1 | async-start | bytes 2097152 | tf_op jit(solution)/shard_map/all_to_all | solution.py:61
  62.3 0.1 copy.22
  62.4 0.0 copy-done
  62.4 3.3 %fusion.2 = f32[32,6,768]{2,0,1:T(8,128)} fusion(bf16[1,2048,768]{2,1,0:T(8,128)(2,1)S(1)} %copy-done, bf16[32,6,2048]{2,1,0:T(8,128)(2,1)} %all-to-all-done.2), kind=kOutput, calls=%fused_computation.12 | convolution fusion | flops 603979776 | bytes 4521984 | tf_op jit(solution)/shard_map/pnd,df->pnf/dot_general | solution.py:12
  65.7 22.9 %all-to-all-done.1 = bf16[32,6,2048]{2,1,0:T(8,128)(2,1)} async-done(((bf16[32,6,2048]{2,1,0:T(8,128)(2,1)}), bf16[32,6,2048]{2,1,0:T(8,128)(2,1)}, u32[]{:S(2)}, u32[]{:S(2)}) %all-to-all-start.1) | async-done | bytes 786464 | tf_op jit(solution)/shard_map/all_to_all | solution.py:61
  88.5 3.7 %fusion.15 = bf16[32,6]{0,1:T(8,128)(2,1)S(1)} fusion(bf16[1,2048,768]{2,1,0:T(8,128)(2,1)} %param.11, bf16[32,6,2048]{2,1,0:T(8,128)(2,1)} %all-to-all-done.1, f32[32,6,768]{2,0,1:T(8,128)} %fusion.2), kind=kOutput, calls=%fused_computation.22 | convolution fusion | flops 605896512 | bytes 4522368 | tf_op jit(solution)/shard_map/pnf,df->pnd/dot_general | solution.py:14
  92.2 0.7 copy.26
  92.9 3.6 %all-to-all-start.4 = ((bf16[32,1,6]{2,1,0:T(2,128)(2,1)}), bf16[32,1,6]{2,1,0:T(2,128)(2,1)S(1)}, u32[]{:S(2)}, u32[]{:S(2)}) async-start(bf16[32,1,6]{2,1,0:T(2,128)(2,1)} %copy.26), calls=%async_computation.4 | async-start | bytes 32768 | tf_op jit(solution)/shard_map/all_to_all | solution.py:69
  96.6 3.6 %fusion.24 = bf16[32,6,768]{2,0,1:T(8,128)(2,1)S(1)} fusion(bf16[1,2048,768]{2,1,0:T(8,128)(2,1)} %param.11, f32[32,6]{0,1:T(8,128)S(1)} %copy.22, f32[32,6,768]{2,0,1:T(8,128)} %fusion.2, bf16[32,6,2048]{2,1,0:T(8,128)(2,1)} %all-to-all-done.1), kind=kOutput, calls=%fused_computation.25 | convolution fusion | flops 606486528 | bytes 4817664 | tf_op jit(solution)/shard_map/pnd,df->pnf/dot_general | solution.py:19
  100.2 1.2 fusion.11
  101.4 1.4 %copy.25 = bf16[32,6,2048]{2,1,0:T(8,128)(2,1)} copy(bf16[32,6,2048]{2,0,1:T(8,128)(2,1)S(1)} %fusion.11) | data formatting | bytes 1572864 | tf_op jit(solution)/shard_map/convert_element_type | solution.py:24
  102.8 0.8 all-to-all-done.4
  103.6 5.3 %all-to-all-start.3 = ((bf16[32,6,2048]{2,1,0:T(8,128)(2,1)}), bf16[32,6,2048]{2,1,0:T(8,128)(2,1)}, u32[]{:S(2)}, u32[]{:S(2)}) async-start(bf16[32,6,2048]{2,1,0:T(8,128)(2,1)} %copy.25), calls=%async_computation.3 | async-start | bytes 2097152 | tf_op jit(solution)/shard_map/all_to_all | solution.py:68
  109.0 0.0 copy-start.1
  109.0 5.5 %bitcast_convert_fusion.3 = f32[1,2048,768]{2,1,0:T(8,128)} fusion(bf16[32,6,768]{2,0,1:T(8,128)(2,1)S(1)} %fusion.24, bf16[32,6,2048]{2,1,0:T(8,128)(2,1)} %all-to-all-done.2), kind=kOutput, calls=%fused_computation.9 | convolution fusion | flops 607125504 | bytes 7372800 | tf_op jit(solution)/shard_map/sc,sf->cf/dot_general | solution.py:85
  114.5 0.0 copy-done.1
  114.5 5.5 %bitcast_convert_fusion.2 = f32[1,2048,768]{2,1,0:T(8,128)} fusion(f32[32,6]{0,1:T(8,128)S(1)} %copy.22, bf16[32,6,2048]{2,1,0:T(8,128)(2,1)} %all-to-all-done.1, f32[32,6,768]{2,0,1:T(8,128)S(1)} %copy-done.1), kind=kOutput, calls=%fused_computation.8 | convolution fusion | flops 609042432 | bytes 7668480 | tf_op jit(solution)/shard_map/sc,sf->cf/dot_general | solution.py:94
  120.0 0.1 reduce
  120.0 0.1 reshape.96
  120.2 1.7 %gather_fusion.2 = bf16[128]{0:T(256)(128)(2,1)} fusion(bf16[192]{0:T(256)(128)(2,1)S(1)} %reshape.96, s32[1024]{0:T(1024)S(1)} %pad_clamp_fusion), kind=kCustom, calls=%fused_computation.4 | custom fusion | bytes 1024 | tf_op jit(solution)/shard_map/gather | solution.py:78
  121.9 13.1 %all-to-all-done.3 = bf16[32,6,2048]{2,1,0:T(8,128)(2,1)} async-done(((bf16[32,6,2048]{2,1,0:T(8,128)(2,1)}), bf16[32,6,2048]{2,1,0:T(8,128)(2,1)}, u32[]{:S(2)}, u32[]{:S(2)}) %all-to-all-start.3) | async-done | bytes 786464 | tf_op jit(solution)/shard_map/all_to_all | solution.py:68
  135.0 2.1 %reshape.95 = bf16[192,2048]{1,0:T(8,128)(2,1)} reshape(bf16[32,6,2048]{2,1,0:T(8,128)(2,1)} %all-to-all-done.3) | data formatting | bytes 1572864 | tf_op jit(solution)/shard_map/reshape | solution.py:71
  137.1 3.5 %gather_fusion.1 = bf16[128,2048]{1,0:T(8,128)(2,1)} fusion(bf16[192,2048]{1,0:T(8,128)(2,1)} %reshape.95, s32[1024]{0:T(1024)S(1)} %pad_clamp_fusion), kind=kCustom, calls=%fused_computation.3 | custom fusion | bytes 1049088 | tf_op jit(solution)/shard_map/gather | solution.py:71
  (6 shorter events, 0.0 us)
Async XLA Ops:
  0.6 61.8 %copy-start = (bf16[1,2048,768]{2,1,0:T(8,128)(2,1)S(1)}, bf16[1,2048,768]{2,1,0:T(8,128)(2,1)}, u32[]{:S(2)}) copy-start(bf16[1,2048,768]{2,1,0:T(8,128)(2,1)} %param.10) | copy-start | bytes 9437188
  6.4 19.9 %all-to-all-start = ((bf16[32,1,6]{2,1,0:T(2,128)(2,1)}), bf16[32,1,6]{2,1,0:T(2,128)(2,1)S(1)}, u32[]{:S(2)}, u32[]{:S(2)}) async-start(bf16[32,1,6]{2,1,0:T(2,128)(2,1)} %convert_element_type.88), calls=%async_computation | async-start | bytes 32768 | tf_op jit(solution)/shard_map/all_to_all | solution.py:62
  26.4 32.2 %all-to-all-start.2 = ((bf16[32,6,2048]{2,1,0:T(8,128)(2,1)}), bf16[32,6,2048]{2,1,0:T(8,128)(2,1)}, u32[]{:S(2)}, u32[]{:S(2)}) async-start(bf16[32,6,2048]{2,1,0:T(8,128)(2,1)} %reshape.94), calls=%async_computation.2 | async-start | bytes 2097152 | tf_op jit(solution)/shard_map/all_to_all | solution.py:60
  58.6 30.0 %all-to-all-start.1 = ((bf16[32,6,2048]{2,1,0:T(8,128)(2,1)}), bf16[32,6,2048]{2,1,0:T(8,128)(2,1)}, u32[]{:S(2)}, u32[]{:S(2)}) async-start(bf16[32,6,2048]{2,1,0:T(8,128)(2,1)} %reshape.93), calls=%async_computation.1 | async-start | bytes 2097152 | tf_op jit(solution)/shard_map/all_to_all | solution.py:61
  92.9 10.7 %all-to-all-start.4 = ((bf16[32,1,6]{2,1,0:T(2,128)(2,1)}), bf16[32,1,6]{2,1,0:T(2,128)(2,1)S(1)}, u32[]{:S(2)}, u32[]{:S(2)}) async-start(bf16[32,1,6]{2,1,0:T(2,128)(2,1)} %copy.26), calls=%async_computation.4 | async-start | bytes 32768 | tf_op jit(solution)/shard_map/all_to_all | solution.py:69
  103.6 31.3 %all-to-all-start.3 = ((bf16[32,6,2048]{2,1,0:T(8,128)(2,1)}), bf16[32,6,2048]{2,1,0:T(8,128)(2,1)}, u32[]{:S(2)}, u32[]{:S(2)}) async-start(bf16[32,6,2048]{2,1,0:T(8,128)(2,1)} %copy.25), calls=%async_computation.3 | async-start | bytes 2097152 | tf_op jit(solution)/shard_map/all_to_all | solution.py:68
  109.0 5.5 %copy-start.1 = (f32[32,6,768]{2,0,1:T(8,128)S(1)}, f32[32,6,768]{2,0,1:T(8,128)}, u32[]{:S(2)}) copy-start(f32[32,6,768]{2,0,1:T(8,128)} %fusion.2) | copy-start | bytes 1769476
where the time goes:
time: 141 us
  waiting for transfers between devices  60.8 us (43%)
  starting transfers between devices  25.9 us (18%)
  local copies, waits for them, and re-layouts  25.1 us (18%)
  matrix products  22.7 us (16%)
  other arithmetic  5.24 us (4%)
    all_to_all x1, waiting for transfers between devices, per_device(): lax.all_to_all(send_tokens, 'expert', split_axis=0, concat_axis=0, tiled=...  24 us
    all_to_all x1, waiting for transfers between devices, per_device(): lax.all_to_all(send_upstream, 'expert', split_axis=0, concat_axis=0, tile...  22.9 us
    all_to_all x1, waiting for transfers between devices, per_device(): lax.all_to_all(row_grad, 'expert', split_axis=0, concat_axis=0, tiled=True)  13.1 us
    all_to_all x1, starting transfers between devices, per_device(): lax.all_to_all(send_gates, 'expert', split_axis=0, concat_axis=0, tiled=T...  7.3 us
    all_to_all x1, starting transfers between devices, per_device(): lax.all_to_all(send_tokens, 'expert', split_axis=0, concat_axis=0, tiled=...  5.96 us
    dot_general x1, matrix products, per_device(): jnp.einsum('sc,sf->cf', columns, flat_hidden, preferred_element_type=jnp....  5.52 us
    dot_general x1, matrix products, per_device(): jnp.einsum('sc,sf->cf', columns, flat_pre, preferred_element_type=jnp.flo...  5.49 us
    all_to_all x1, starting transfers between devices, per_device(): lax.all_to_all(row_grad, 'expert', split_axis=0, concat_axis=0, tiled=True)  5.31 us
  transfers between devices with their start and end apart: 5, of which 4 were waited for; matrix products, arithmetic and copies ran while one was open for 27% of the time, Pallas kernels for 0%

commit v1 on v0

v1 whole, which is shorter than its diff:
```python
import functools
import math

import jax
import jax.numpy as jnp
from jax import lax
from jax.experimental import pallas as pl
from jax.experimental.pallas import tpu as pltpu
from jax.sharding import PartitionSpec as P

GATE_DEN = 256
LANES = 128
BF16 = jnp.bfloat16
F32 = jnp.float32
MESH = pl.DeviceIdType.MESH


def dot(a, b, dims=((1,), (0,))):
    return lax.dot_general(a, b, (dims, ((), ())), preferred_element_type=F32)


def swap_matrix(fold, cap):
    side = fold * fold * cap
    row = lax.broadcasted_iota(jnp.int32, (side, LANES), 0).astype(F32)
    a = jnp.floor((row + 0.5) * (1.0 / (fold * cap)))
    rest = row - a * (fold * cap)
    b = jnp.floor((rest + 0.5) * (1.0 / cap))
    s = rest - b * cap
    source = (b * (fold * cap) + a * cap + s).astype(jnp.int32)
    lane = lax.broadcasted_iota(jnp.int32, (side, LANES), 1)
    parts = []
    for start in range(0, side, LANES):
        parts.append(jnp.where(source == lane + start, 1.0, 0.0).astype(BF16))
    return jnp.concatenate(parts, axis=1)


def slot_one_hot(routes_row, cap, slots):
    count = routes_row.shape[1]
    along = jnp.broadcast_to(routes_row.astype(F32), (count, count))
    down = along.T
    i = lax.broadcasted_iota(jnp.int32, (count, count), 0)
    j = lax.broadcasted_iota(jnp.int32, (count, count), 1)
    rank = jnp.sum(jnp.where((along == down) & (i < j), 1.0, 0.0), axis=0, keepdims=True)
    slot = (routes_row.astype(F32) * cap + rank).astype(jnp.int32)
    number = lax.broadcasted_iota(jnp.int32, (slots, count), 0)
    return jnp.where(number == slot, 1.0, 0.0).astype(BF16)


def spread_matrix(devices, cap, pad):
    rows, columns = devices * pad, devices * cap
    row = lax.broadcasted_iota(jnp.int32, (rows, columns), 0).astype(F32)
    lane = lax.broadcasted_iota(jnp.int32, (rows, columns), 1).astype(F32)
    d = jnp.floor((row + 0.5) * (1.0 / pad))
    s = row - d * pad
    return jnp.where((s < cap) & (d * cap + s == lane), 1.0, 0.0).astype(BF16)


def prepare_kernel(fold, cap, tokens, upstream, routes, shares, send):
    devices, block, width = send.shape
    chunk = width // 2
    count, features = tokens.shape
    gate = jnp.broadcast_to(shares[...].astype(F32) * (1.0 / GATE_DEN), (count, count)).T
    one_hot = slot_one_hot(routes[...], cap, devices * cap)
    swap = swap_matrix(fold, cap)
    scaled = jnp.concatenate(
        [
            (upstream[:, at : at + count].astype(F32) * gate).astype(BF16)
            for at in range(0, features, count)
        ],
        axis=1,
    )
    sent_tokens = dot(one_hot, tokens[...]).astype(BF16)
    sent_scaled = dot(one_hot, scaled).astype(BF16)
    for group in range(devices // fold):
        rows = slice(group * block, (group + 1) * block)
        for half, rows_of in enumerate((sent_tokens, sent_scaled)):
            stacked = jnp.concatenate(
                [rows_of[rows, c * chunk : (c + 1) * chunk] for c in range(fold)], axis=0
            )
            folded = dot(swap, stacked).astype(BF16)
            send[group * fold : (group + 1) * fold, :, half * chunk : (half + 1) * chunk] = (
                folded.reshape(fold, block, chunk)
            )


def exchange_kernel(devices, arrays, *refs):
    sources, targets = refs[:arrays], refs[arrays : 2 * arrays]
    send_sem, recv_sem, own_sem = refs[2 * arrays :]
    me = lax.axis_index("expert")
    barrier = pltpu.get_barrier_semaphore()

    def greet(step, carry):
        pl.semaphore_signal(
            barrier, inc=1, device_id={"expert": lax.rem(me + step, devices)}, device_id_type=MESH
        )
        return carry

    lax.fori_loop(1, devices, greet, 0)
    pl.semaphore_wait(barrier, devices - 1)

    def remote(step, k):
        to = lax.rem(me + step, devices)
        return pltpu.make_async_remote_copy(
            src_ref=sources[k].at[to],
            dst_ref=targets[k].at[me],
            send_sem=send_sem.at[k, step],
            recv_sem=recv_sem.at[k, step],
            device_id={"expert": to},
            device_id_type=MESH,
        )

    def arrival(step, k):
        came = lax.rem(me + devices - step, devices)
        return pltpu.make_async_remote_copy(
            src_ref=sources[k].at[came],
            dst_ref=targets[k].at[came],
            send_sem=send_sem.at[k, step],
            recv_sem=recv_sem.at[k, step],
            device_id={"expert": came},
            device_id_type=MESH,
        )

    def start(step, carry):
        for k in range(arrays):
            remote(step, k).start()
        return carry

    def finish(step, carry):
        for k in range(arrays):
            remote(step, k).wait_send()
            arrival(step, k).wait_recv()
        return carry

    lax.fori_loop(1, devices, start, 0)
    for k in range(arrays):
        own = pltpu.make_async_copy(sources[k].at[me], targets[k].at[me], own_sem.at[k])
        own.start()
        own.wait()
    lax.fori_loop(1, devices, finish, 0)


def exchange(collective_id, *arrays):
    devices = arrays[0].shape[0]
    count = len(arrays)
    return pl.pallas_call(
        functools.partial(exchange_kernel, devices, count),
        out_shape=[jax.ShapeDtypeStruct(a.shape, a.dtype) for a in arrays],
        in_specs=[pl.BlockSpec(memory_space=pl.ANY)] * count,
        out_specs=[pl.BlockSpec(memory_space=pl.ANY)] * count,
        scratch_shapes=[
            pltpu.SemaphoreType.DMA((count, devices)),
            pltpu.SemaphoreType.DMA((count, devices)),
            pltpu.SemaphoreType.DMA((count,)),
        ],
        compiler_params=pltpu.CompilerParams(
            collective_id=collective_id, has_side_effects=True, vmem_limit_bytes=1 << 20
        ),
    )(*arrays)


def unfold(swap, blocks, fold, first, chunk):
    part = blocks[:, :, first : first + chunk]
    return dot(swap, part.reshape(part.shape[0] * part.shape[1], chunk)).astype(BF16)


def expert_kernel(fold, cap, got, w_up, w_down, tokens, scaled, hidden_out, pre_grad_out, back, back_q):
    devices, block, width = got.shape
    chunk = width // 2
    pad = back_q.shape[1]
    swap = swap_matrix(fold, cap)
    for group in range(devices // fold):
        blocks = got[group * fold : (group + 1) * fold]
        for half, out in enumerate((tokens, scaled)):
            rows = unfold(swap, blocks, fold, half * chunk, chunk)
            for c in range(fold):
                out[group * block : (group + 1) * block, c * chunk : (c + 1) * chunk] = rows[
                    c * block : (c + 1) * block
                ]
    pre = dot(tokens[...], w_up[0])
    cotangent = dot(scaled[...], w_down[0])
    sigmoid = jax.nn.sigmoid(pre)
    hidden = (pre * sigmoid).astype(BF16)
    pre_grad = (cotangent * sigmoid * (1.0 + pre * (1.0 - sigmoid))).astype(BF16)
    hidden_out[...] = hidden
    pre_grad_out[...] = pre_grad
    gate_sum = jnp.sum(hidden.astype(F32) * cotangent, axis=1, keepdims=True)
    gate_rows = jnp.broadcast_to(gate_sum, (devices * cap, LANES)).astype(BF16)
    back_q[...] = (
        dot(spread_matrix(devices, cap, pad), gate_rows).astype(BF16).reshape(devices, pad, LANES)
    )
    row_grad = dot(pre_grad, w_up[0], ((1,), (1,))).astype(BF16)
    for group in range(devices // fold):
        rows = slice(group * block, (group + 1) * block)
        stacked = jnp.concatenate(
            [row_grad[rows, c * chunk : (c + 1) * chunk] for c in range(fold)], axis=0
        )
        back[group * fold : (group + 1) * fold] = (
            dot(swap, stacked).astype(BF16).reshape(fold, block, chunk)
        )


def return_kernel(fold, cap, back, back_q, routes, shares, token_grad, gate_grad, rows_ref):
    devices, block, chunk = back.shape
    pad = back_q.shape[1]
    swap = swap_matrix(fold, cap)
    one_hot = slot_one_hot(routes[...], cap, devices * cap)
    for group in range(devices // fold):
        rows = unfold(swap, back[group * fold : (group + 1) * fold], fold, 0, chunk)
        for c in range(fold):
            rows_ref[group * block : (group + 1) * block, c * chunk : (c + 1) * chunk] = rows[
                c * block : (c + 1) * block
            ]
    token_grad[...] = dot(one_hot, rows_ref[...], ((0,), (0,))).astype(BF16)
    spread = spread_matrix(devices, cap, pad)
    sums = dot(spread, back_q[...].reshape(devices * pad, LANES), ((0,), (0,))).astype(BF16)
    per_token = dot(sums, one_hot, ((0,), (0,)))[0:1]
    gate_grad[...] = (per_token / (shares[...].astype(F32) * (1.0 / GATE_DEN))).astype(BF16)


def weight_kernel(tokens, scaled, hidden, pre_grad, up_grad, down_grad):
    up = dot(tokens[...], pre_grad[...], ((0,), (0,))).astype(BF16)
    down = dot(scaled[...], hidden[...], ((0,), (0,))).astype(BF16)
    up_grad[...] = up.astype(up_grad.dtype)[None]
    down_grad[...] = down.astype(down_grad.dtype)[None]


def per_device(tokens, upstream, w_up, w_down, routes, gate_share):
    count, features = tokens.shape
    units = w_up.shape[2]
    devices = lax.axis_size("expert")
    groups = lax.axis_size("dp")
    cap = (3 * count + 2 * devices - 1) // (2 * devices)
    fold = 16 // math.gcd(16, cap)
    block, chunk = fold * cap, features // fold
    slots = devices * cap
    routes_row, shares_row = routes.reshape(1, count), gate_share.reshape(1, count)
    roomy = pltpu.CompilerParams(vmem_limit_bytes=48 << 20)
    send = pl.pallas_call(
        functools.partial(prepare_kernel, fold, cap),
        out_shape=jax.ShapeDtypeStruct((devices, block, 2 * chunk), BF16),
        compiler_params=roomy,
    )(tokens, upstream, routes_row, shares_row)
    (got,) = exchange(1, send)
    got_tokens, got_scaled, hidden, pre_grad, back, back_q = pl.pallas_call(
        functools.partial(expert_kernel, fold, cap),
        out_shape=[
            jax.ShapeDtypeStruct((slots, features), BF16),
            jax.ShapeDtypeStruct((slots, features), BF16),
            jax.ShapeDtypeStruct((slots, units), BF16),
            jax.ShapeDtypeStruct((slots, units), BF16),
            jax.ShapeDtypeStruct((devices, block, chunk), BF16),
            jax.ShapeDtypeStruct((devices, 16, LANES), BF16),
        ],
        compiler_params=roomy,
    )(got, w_up, w_down)
    back, back_q = exchange(2, back, back_q)
    token_grad, gate_grad = pl.pallas_call(
        functools.partial(return_kernel, fold, cap),
        out_shape=[
            jax.ShapeDtypeStruct((count, features), BF16),
            jax.ShapeDtypeStruct((1, count), BF16),
        ],
        scratch_shapes=[pltpu.VMEM((slots, features), BF16)],
        compiler_params=roomy,
    )(back, back_q, routes_row, shares_row)
    tile = 256
    kind = F32 if groups == 1 else BF16
    up_grad, down_grad = pl.pallas_call(
        weight_kernel,
        grid=(features // tile,),
        in_specs=[
            pl.BlockSpec((slots, tile), lambda i: (0, i)),
            pl.BlockSpec((slots, tile), lambda i: (0, i)),
            pl.BlockSpec((slots, units), lambda i: (0, 0)),
            pl.BlockSpec((slots, units), lambda i: (0, 0)),
        ],
        out_specs=[pl.BlockSpec((1, tile, units), lambda i: (0, i, 0))] * 2,
        out_shape=[jax.ShapeDtypeStruct((1, features, units), kind)] * 2,
        compiler_params=roomy,
    )(got_tokens, got_scaled, hidden, pre_grad)
    if groups > 1:
        up_grad, down_grad = (
            lax.psum_scatter(g, "dp", scatter_dimension=1, tiled=True).astype(F32)
            for g in (up_grad, down_grad)
        )
    return token_grad, gate_grad.reshape(count, 1), up_grad, down_grad


def solution(mesh):
    rows, experts = P(("dp", "expert"), None), P("expert", None, None)
    return jax.shard_map(
        per_device,
        mesh=mesh,
        in_specs=(rows, rows, experts, experts, rows, rows),
        out_specs=(rows, rows, P("expert", "dp", None), P("expert", "dp", None)),
        check_vma=False,
    )
```

time: 141 us -> 89.2 us (0.63)
  the two profiles are of different devices: /device:TPU:0 before, /device:TPU:15 now
where the time goes in v1:
time: 89.2 us; the launch traced here: 89 us
  Pallas kernels  84.9 us (95%)
  local copies, waits for them, and re-layouts  3.39 us (4%)
    pallas_call x2, Pallas kernels, exchange(): pl.pallas_call(functools.partial(exchange_kernel, devices, count), out_sh...  68.5 us
    pallas_call x1, Pallas kernels, per_device(): pl.pallas_call(functools.partial(expert_kernel, fold, cap), out_shape=[ja...  6.81 us
    pallas_call x1, Pallas kernels, per_device(): pl.pallas_call(weight_kernel, grid=(features // tile,), in_specs=[pl.Bloc...  6.46 us
    unnamed x8, local copies, waits for them, and re-layouts  3.39 us

profile of v1, /device:TPU:15, one launch (start us, length us, event | category | flops | bytes accessed | tf_op | source)
XLA Modules:
  0.0 89.0 jit_solution(1402046363338620466)
XLA Ops:
  0.6 0.0 copy-start
  0.6 1.0 %copy-done = bf16[128,2048]{1,0:T(8,128)(2,1)S(1)} copy-done((bf16[128,2048]{1,0:T(8,128)(2,1)S(1)}, bf16[128,2048]{1,0:T(8,128)(2,1)}, u32[]{:S(2)}) %copy-start) | copy-done | bytes 524312
  1.7 0.0 copy-start.1
  1.7 1.0 %copy-done.1 = bf16[128,2048]{1,0:T(8,128)(2,1)S(1)} copy-done((bf16[128,2048]{1,0:T(8,128)(2,1)S(1)}, bf16[128,2048]{1,0:T(8,128)(2,1)}, u32[]{:S(2)}) %copy-start.1) | copy-done | bytes 524312
  2.7 0.0 copy-start.2
  2.7 0.7 copy-done.2
  3.4 0.0 copy-start.3
  3.4 0.7 copy-done.3
  4.0 1.5 %shard_map.93.refs_0_ = bf16[32,48,512]{2,1,0:T(8,128)(2,1)S(1)} custom-call(bf16[128,2048]{1,0:T(8,128)(2,1)S(1)} %copy-done, bf16[128,2048]{1,0:T(8,128)(2,1)S(1)} %copy-done.1, s32[1,128]{1,0:T(1,128)S(1)} %bitcast.3, s32[1,128]{1,0:T(1,128)S(1)} %bitcast.5), custom_call_target="tpu_custom_call" | custom-call | tf_op jit(solution)/shard_map/pallas_call | solution.py:238
  5.6 42.5 %shard_map.94.got = bf16[32,48,512]{2,1,0:T(8,128)(2,1)S(1)} custom-call(bf16[32,48,512]{2,1,0:T(8,128)(2,1)S(1)} %shard_map.93.refs_0_), custom_call_target="tpu_custom_call" | custom-call | tf_op jit(solution)/shard_map/pallas_call | solution.py:145
  48.1 6.8 %shard_map.95 = (bf16[192,2048]{1,0:T(8,128)(2,1)S(1)}, bf16[192,2048]{1,0:T(8,128)(2,1)S(1)}, bf16[192,768]{1,0:T(8,128)(2,1)S(1)}, bf16[192,768]{1,0:T(8,128)(...) custom-call(bf16[32,48,512]{2,1,0:T(8,128)(2,1)S(1)} %shard_map.94.got, ...), custom_call_target="tpu_custom_call" | custom-call | tf_op jit(solution)/shard_map/pallas_call | solution.py:244
  54.9 26.0 %shard_map.96 = (bf16[32,48,256]{2,1,0:T(8,128)(2,1)S(1)}, bf16[32,16,128]{2,1,0:T(8,128)(2,1)S(1)}) custom-call(bf16[32,48,256]{2,1,0:T(8,128)(2,1)S(1)} %get-tuple-element.16.refs_0_, bf16[32,16,128]{2,1,0:T(8,128)(2,1)S(1)} %get-tuple-element.17.refs_1_), custom_call_target="tpu_custom_call" | custom-call | tf_op jit(solution)/shard_map/pallas_call | solution.py:145
  80.9 1.6 %shard_map.97 = (bf16[128,2048]{1,0:T(8,128)(2,1)}, bf16[1,128]{1,0:T(2,128)(2,1)}) custom-call(bf16[32,48,256]{2,1,0:T(8,128)(2,1)S(1)} %get-tuple-element.18.back, bf16[32,16,128]{2,1,0:T(8,128)(2,1)S(1)} %get-tuple-element.19.back_q, s32[1,128]{1,0:T(1,128)S(1)} %bitcast.4, s32[1,128]{1,0:T(1,128)S(1)} %bitcast.6), custom_call_target="tpu_custom_call" | custom-call | tf_op jit(solution)/shard_map/pallas_call | solution.py:257
  82.5 6.5 %shard_map.98 = (f32[1,2048,768]{2,1,0:T(8,128)}, f32[1,2048,768]{2,1,0:T(8,128)}) custom-call(bf16[192,2048]{1,0:T(8,128)(2,1)S(1)} %get-tuple-element.22.tokens, bf16[192,2048]{1,0:T(8,128)(2,1)S(1)} %get-tuple-element.23.scaled, bf16[192,768]{1,0:T(8,128)(2,1)S(1)} %get-tuple-element.24.hidden, bf16[192,768]{1,0:T(8,128)(2,1)S(1)} %get-tuple-element.25.pre_grad), custom_call_target="tpu_custom_call" | custom-call | tf_op jit(solution)/shard_map/pallas_call | solution.py:268
Async XLA Ops:
  0.6 1.0 %copy-start = (bf16[128,2048]{1,0:T(8,128)(2,1)S(1)}, bf16[128,2048]{1,0:T(8,128)(2,1)}, u32[]{:S(2)}) copy-start(bf16[128,2048]{1,0:T(8,128)(2,1)} %tokens.1) | copy-start | bytes 1572868
  1.7 1.0 %copy-start.1 = (bf16[128,2048]{1,0:T(8,128)(2,1)S(1)}, bf16[128,2048]{1,0:T(8,128)(2,1)}, u32[]{:S(2)}) copy-start(bf16[128,2048]{1,0:T(8,128)(2,1)} %upstream.1) | copy-start | bytes 1572868
  2.7 0.7 copy-start.2
  3.4 0.7 copy-start.3

commit v2 on v1

v2 whole, which is shorter than its diff:
```python
import functools
import math

import jax
import jax.numpy as jnp
from jax import lax
from jax.experimental import pallas as pl
from jax.experimental.pallas import tpu as pltpu
from jax.sharding import PartitionSpec as P

GATE_DEN = 256
LANES = 128
BF16 = jnp.bfloat16
F32 = jnp.float32
MESH = pl.DeviceIdType.MESH


def dot(a, b, dims=((1,), (0,))):
    return lax.dot_general(a, b, (dims, ((), ())), preferred_element_type=F32)


def swap_matrix(fold, cap):
    side = fold * fold * cap
    row = lax.broadcasted_iota(jnp.int32, (side, LANES), 0).astype(F32)
    a = jnp.floor((row + 0.5) * (1.0 / (fold * cap)))
    rest = row - a * (fold * cap)
    b = jnp.floor((rest + 0.5) * (1.0 / cap))
    s = rest - b * cap
    source = (b * (fold * cap) + a * cap + s).astype(jnp.int32)
    lane = lax.broadcasted_iota(jnp.int32, (side, LANES), 1)
    parts = []
    for start in range(0, side, LANES):
        parts.append(jnp.where(source == lane + start, 1.0, 0.0).astype(BF16))
    return jnp.concatenate(parts, axis=1)


def slot_one_hot(routes_row, cap, slots):
    count = routes_row.shape[1]
    along = jnp.broadcast_to(routes_row.astype(F32), (count, count))
    down = along.T
    i = lax.broadcasted_iota(jnp.int32, (count, count), 0)
    j = lax.broadcasted_iota(jnp.int32, (count, count), 1)
    rank = jnp.sum(jnp.where((along == down) & (i < j), 1.0, 0.0), axis=0, keepdims=True)
    slot = (routes_row.astype(F32) * cap + rank).astype(jnp.int32)
    number = lax.broadcasted_iota(jnp.int32, (slots, count), 0)
    return jnp.where(number == slot, 1.0, 0.0).astype(BF16)


def pick_matrices(devices, cap):
    slots = devices * cap
    d = lax.broadcasted_iota(jnp.int32, (devices, slots), 0).astype(F32)
    slot = lax.broadcasted_iota(jnp.int32, (devices, slots), 1).astype(F32)
    owner = jnp.where(jnp.floor((slot + 0.5) * (1.0 / cap)) == d, 1.0, 0.0)
    slot = lax.broadcasted_iota(jnp.int32, (slots, LANES), 0).astype(F32)
    lane = lax.broadcasted_iota(jnp.int32, (slots, LANES), 1).astype(F32)
    rank = slot - jnp.floor((slot + 0.5) * (1.0 / cap)) * cap
    return owner, jnp.where(rank == lane, 1.0, 0.0)


def fold_rows(swap, rows_of, out, fold):
    devices, block, chunk = out.shape
    for group in range(devices // fold):
        rows = slice(group * block, (group + 1) * block)
        stacked = jnp.concatenate(
            [rows_of[rows, c * chunk : (c + 1) * chunk] for c in range(fold)], axis=0
        )
        out[group * fold : (group + 1) * fold] = (
            dot(swap, stacked).astype(BF16).reshape(fold, block, chunk)
        )


def unfold_rows(swap, blocks, out, fold):
    devices, block, chunk = blocks.shape
    for group in range(devices // fold):
        part = blocks[group * fold : (group + 1) * fold]
        rows = dot(swap, part.reshape(fold * block, chunk)).astype(BF16)
        for c in range(fold):
            out[group * block : (group + 1) * block, c * chunk : (c + 1) * chunk] = rows[
                c * block : (c + 1) * block
            ]


def layer_kernel(
    fold,
    cap,
    tokens,
    upstream,
    routes,
    shares,
    w_up_hbm,
    w_down_hbm,
    tokens_t,
    scaled_t,
    hidden_out,
    pre_grad_out,
    token_grad,
    gate_grad,
    w_up,
    w_down,
    send_tokens,
    send_scaled,
    got_tokens,
    got_scaled,
    send_back,
    got_back,
    send_sums,
    got_sums,
    rows_ref,
    send_sem,
    recv_sem,
    own_sem,
    weight_sem,
):
    devices, block, chunk = send_tokens.shape
    half = devices // 2
    count, features = tokens.shape
    slots = devices * cap
    me = lax.axis_index("expert")
    place = lax.rem(me, half)
    near = me - place
    far = half - near
    channels = (
        (send_tokens, got_tokens),
        (send_scaled, got_scaled),
        (send_back, got_back),
        (send_sums, got_sums),
    )

    up_copy = pltpu.make_async_copy(w_up_hbm.at[0], w_up, weight_sem.at[0])
    down_copy = pltpu.make_async_copy(w_down_hbm.at[0], w_down, weight_sem.at[1])
    up_copy.start()
    down_copy.start()

    barrier = pltpu.get_barrier_semaphore()

    def greet(step, carry):
        pl.semaphore_signal(
            barrier, inc=1, device_id={"expert": lax.rem(me + step, devices)}, device_id_type=MESH
        )
        return carry

    lax.fori_loop(1, devices, greet, 0)

    def copy(k, base, first, step, peer):
        source, target = channels[k]
        return pltpu.make_async_remote_copy(
            src_ref=source.at[peer],
            dst_ref=target.at[me],
            send_sem=send_sem.at[k, first + step],
            recv_sem=recv_sem.at[k, first + step],
            device_id={"expert": peer},
            device_id_type=MESH,
        )

    def push(k, across, step):
        base, first = (far, 0) if across else (near, half)
        peer = base + lax.rem(place + step, half)
        copy(k, base, first, step, peer).start()

    def send_all(k):
        def across(step, carry):
            push(k, True, step)
            return carry

        def within(step, carry):
            push(k, False, step)
            return carry

        lax.fori_loop(0, half, across, 0)
        lax.fori_loop(1, half, within, 0)
        source, target = channels[k]
        pltpu.make_async_copy(source.at[me], target.at[me], own_sem.at[k]).start()

    def drain(k):
        source, target = channels[k]

        def one(first, base, step):
            peer = base + lax.rem(place + step, half)
            copy(k, base, first, step, peer).wait_send()
            came = base + lax.rem(place + half - step, half)
            pltpu.make_async_remote_copy(
                src_ref=source.at[came],
                dst_ref=target.at[came],
                send_sem=send_sem.at[k, first + step],
                recv_sem=recv_sem.at[k, first + step],
                device_id={"expert": came},
                device_id_type=MESH,
            ).wait_recv()

        def across(step, carry):
            one(0, far, step)
            return carry

        def within(step, carry):
            one(half, near, step)
            return carry

        lax.fori_loop(0, half, across, 0)
        lax.fori_loop(1, half, within, 0)
        pltpu.make_async_copy(source.at[me], target.at[me], own_sem.at[k]).wait()

    swap = swap_matrix(fold, cap)
    one_hot = slot_one_hot(routes[...], cap, slots)
    fold_rows(swap, dot(one_hot, tokens[...]).astype(BF16), send_tokens, fold)
    pl.semaphore_wait(barrier, devices - 1)
    send_all(0)
    gate_row = shares[...].astype(F32) * (1.0 / GATE_DEN)
    gate = jnp.broadcast_to(gate_row, (count, count)).T
    scaled = jnp.concatenate(
        [
            (upstream[:, at : at + count].astype(F32) * gate).astype(BF16)
            for at in range(0, features, count)
        ],
        axis=1,
    )
    fold_rows(swap, dot(one_hot, scaled).astype(BF16), send_scaled, fold)
    send_all(1)

    owner, rank = pick_matrices(devices, cap)
    up_copy.wait()
    drain(0)
    unfold_rows(swap, got_tokens, rows_ref, fold)
    pre = dot(rows_ref[...], w_up[...])
    sigmoid = jax.nn.sigmoid(pre)
    hidden = (pre * sigmoid).astype(BF16)
    slope = sigmoid * (1.0 + pre * (1.0 - sigmoid))
    hidden_out[...] = hidden
    tokens_t[...] = rows_ref[...].T

    down_copy.wait()
    drain(1)
    unfold_rows(swap, got_scaled, rows_ref, fold)
    cotangent = dot(rows_ref[...], w_down[...])
    pre_grad = (cotangent * slope).astype(BF16)
    row_grad = dot(pre_grad, w_up[...], ((1,), (1,))).astype(BF16)
    fold_rows(swap, row_grad, send_back, fold)
    send_all(2)
    sums = jnp.sum(hidden.astype(F32) * cotangent, axis=1, keepdims=True).astype(BF16).astype(F32)
    send_sums[...] = dot(owner.astype(BF16), (sums * rank).astype(BF16)).reshape(devices, 1, LANES)
    send_all(3)
    pre_grad_out[...] = pre_grad
    scaled_t[...] = rows_ref[...].T

    drain(3)
    picked = dot(owner.astype(BF16), got_sums[...].reshape(devices, LANES).astype(BF16), ((0,), (0,)))
    picked = jnp.sum(picked * rank, axis=1, keepdims=True)
    per_token = jnp.sum(picked * one_hot.astype(F32), axis=0, keepdims=True)
    gate_grad[...] = (per_token / gate_row).astype(BF16)
    drain(2)
    unfold_rows(swap, got_back, rows_ref, fold)
    token_grad[...] = dot(one_hot, rows_ref[...], ((0,), (0,))).astype(BF16)


def weight_kernel(tokens_t, scaled_t, hidden, pre_grad, up_grad, down_grad):
    up = dot(tokens_t[...], pre_grad[...]).astype(BF16)
    down = dot(scaled_t[...], hidden[...]).astype(BF16)
    up_grad[...] = up.astype(up_grad.dtype)[None]
    down_grad[...] = down.astype(down_grad.dtype)[None]


def per_device(tokens, upstream, w_up, w_down, routes, gate_share):
    count, features = tokens.shape
    units = w_up.shape[2]
    devices = lax.axis_size("expert")
    groups = lax.axis_size("dp")
    cap = (3 * count + 2 * devices - 1) // (2 * devices)
    fold = 16 // math.gcd(16, cap)
    block, chunk = fold * cap, features // fold
    slots = devices * cap
    routes_row, shares_row = routes.reshape(1, count), gate_share.reshape(1, count)
    roomy = pltpu.CompilerParams(vmem_limit_bytes=48 << 20)
    rows = jax.ShapeDtypeStruct((features, slots), BF16)
    units_of = jax.ShapeDtypeStruct((slots, units), BF16)
    whole, outside = pl.BlockSpec(memory_space=pltpu.VMEM), pl.BlockSpec(memory_space=pl.ANY)
    buffer = pltpu.VMEM((devices, block, chunk), BF16)
    sums = pltpu.VMEM((devices, 1, LANES), F32)
    tokens_t, scaled_t, hidden, pre_grad, token_grad, gate_grad = pl.pallas_call(
        functools.partial(layer_kernel, fold, cap),
        in_specs=[whole] * 4 + [outside] * 2,
        out_specs=[whole] * 6,
        out_shape=[
            rows,
            rows,
            units_of,
            units_of,
            jax.ShapeDtypeStruct((count, features), BF16),
            jax.ShapeDtypeStruct((1, count), BF16),
        ],
        scratch_shapes=[
            pltpu.VMEM((features, units), BF16),
            pltpu.VMEM((features, units), BF16),
            *([buffer] * 6),
            sums,
            sums,
            pltpu.VMEM((slots, features), BF16),
            pltpu.SemaphoreType.DMA((4, devices)),
            pltpu.SemaphoreType.DMA((4, devices)),
            pltpu.SemaphoreType.DMA((4,)),
            pltpu.SemaphoreType.DMA((2,)),
        ],
        compiler_params=pltpu.CompilerParams(
            collective_id=1, has_side_effects=True, vmem_limit_bytes=48 << 20
        ),
    )(tokens, upstream, routes_row, shares_row, w_up, w_down)
    tile = 256
    kind = F32 if groups == 1 else BF16
    up_grad, down_grad = pl.pallas_call(
        weight_kernel,
        grid=(features // tile,),
        in_specs=[
            pl.BlockSpec((tile, slots), lambda i: (i, 0)),
            pl.BlockSpec((tile, slots), lambda i: (i, 0)),
            pl.BlockSpec((slots, units), lambda i: (0, 0)),
            pl.BlockSpec((slots, units), lambda i: (0, 0)),
        ],
        out_specs=[pl.BlockSpec((1, tile, units), lambda i: (0, i, 0))] * 2,
        out_shape=[jax.ShapeDtypeStruct((1, features, units), kind)] * 2,
        compiler_params=roomy,
    )(tokens_t, scaled_t, hidden, pre_grad)
    if groups > 1:
        up_grad, down_grad = (
            lax.psum_scatter(g, "dp", scatter_dimension=1, tiled=True).astype(F32)
            for g in (up_grad, down_grad)
        )
    return token_grad, gate_grad.reshape(count, 1), up_grad, down_grad


def solution(mesh):
    rows, experts = P(("dp", "expert"), None), P("expert", None, None)
    return jax.shard_map(
        per_device,
        mesh=mesh,
        in_specs=(rows, rows, experts, experts, rows, rows),
        out_specs=(rows, rows, P("expert", "dp", None), P("expert", "dp", None)),
        check_vma=False,
    )
```

time: 89.2 us -> 80.5 us (0.902)
  the two profiles are of different devices: /device:TPU:15 before, /device:TPU:0 now
where the time goes in v2:
time: 80.5 us; the launch traced here: 80.3 us
  Pallas kernels  75 us (93%)
  local copies, waits for them, and re-layouts  4.69 us (6%)
    pallas_call x1, Pallas kernels, per_device(): pl.pallas_call(functools.partial(layer_kernel, fold, cap), in_specs=[whol...  68.8 us
    pallas_call x1, Pallas kernels, per_device(): pl.pallas_call(weight_kernel, grid=(features // tile,), in_specs=[pl.Bloc...  6.21 us
    unnamed x10, local copies, waits for them, and re-layouts  4.69 us

profile of v2, /device:TPU:0, one launch (start us, length us, event | category | flops | bytes accessed | tf_op | source)
XLA Modules:
  0.0 80.3 jit_solution(17624380675110961134)
XLA Ops:
  0.6 0.0 copy-start
  0.6 1.0 %copy-done = bf16[128,2048]{1,0:T(8,128)(2,1)S(1)} copy-done((bf16[128,2048]{1,0:T(8,128)(2,1)S(1)}, bf16[128,2048]{1,0:T(8,128)(2,1)}, u32[]{:S(2)}) %copy-start) | copy-done | bytes 524312
  1.7 0.0 copy-start.1
  1.7 1.0 %copy-done.1 = bf16[128,2048]{1,0:T(8,128)(2,1)S(1)} copy-done((bf16[128,2048]{1,0:T(8,128)(2,1)S(1)}, bf16[128,2048]{1,0:T(8,128)(2,1)}, u32[]{:S(2)}) %copy-start.1) | copy-done | bytes 524312
  2.7 0.0 copy-start.2
  2.7 0.7 copy-done.2
  3.4 0.0 copy-start.3
  3.4 0.7 copy-done.3
  4.0 68.8 %shard_map.93 = (bf16[2048,192]{1,0:T(8,128)(2,1)S(1)}, bf16[2048,192]{1,0:T(8,128)(2,1)S(1)}, bf16[192,768]{1,0:T(8,128)(2,1)S(1)}, bf16[192,768]{1,0:T(8,128)(...) custom-call(bf16[128,2048]{1,0:T(8,128)(2,1)S(1)} %copy-done, bf16[128,2048]{1,0:T(8,128)(2,1)S(1)} %copy-done.1, ...), custom_call_target="tpu_custom_call" | custom-call | tf_op jit(solution)/shard_map/pallas_call | solution.py:277
  72.8 6.2 %shard_map.94 = (f32[1,2048,768]{2,1,0:T(8,128)}, f32[1,2048,768]{2,1,0:T(8,128)}) custom-call(bf16[2048,192]{1,0:T(8,128)(2,1)S(1)} %get-tuple-element.14.tokens_t, bf16[2048,192]{1,0:T(8,128)(2,1)S(1)} %get-tuple-element.15.scaled_t, bf16[192,768]{1,0:T(8,128)(2,1)S(1)} %get-tuple-element.16.hidden, bf16[192,768]{1,0:T(8,128)(2,1)S(1)} %get-tuple-element.17.pre_grad), custom_call_target="tpu_custom_call" | custom-call | tf_op jit(solution)/shard_map/pallas_call | solution.py:307
  79.0 0.8 copy.12
  79.8 0.5 copy.13
Async XLA Ops:
  0.6 1.0 %copy-start = (bf16[128,2048]{1,0:T(8,128)(2,1)S(1)}, bf16[128,2048]{1,0:T(8,128)(2,1)}, u32[]{:S(2)}) copy-start(bf16[128,2048]{1,0:T(8,128)(2,1)} %tokens.1) | copy-start | bytes 1572868
  1.7 1.0 %copy-start.1 = (bf16[128,2048]{1,0:T(8,128)(2,1)S(1)}, bf16[128,2048]{1,0:T(8,128)(2,1)}, u32[]{:S(2)}) copy-start(bf16[128,2048]{1,0:T(8,128)(2,1)} %upstream.1) | copy-start | bytes 1572868
  2.7 0.7 copy-start.2
  3.4 0.7 copy-start.3

commit v3 on v2

v3 whole, which is shorter than its diff:
```python
import functools
import math

import jax
import jax.numpy as jnp
from jax import lax
from jax.experimental import pallas as pl
from jax.experimental.pallas import tpu as pltpu
from jax.sharding import PartitionSpec as P

GATE_DEN = 256
LANES = 128
BF16 = jnp.bfloat16
F32 = jnp.float32
MESH = pl.DeviceIdType.MESH


def dot(a, b, dims=((1,), (0,))):
    return lax.dot_general(a, b, (dims, ((), ())), preferred_element_type=F32)


def swap_matrix(fold, cap):
    side = fold * fold * cap
    row = lax.broadcasted_iota(jnp.int32, (side, LANES), 0).astype(F32)
    a = jnp.floor((row + 0.5) * (1.0 / (fold * cap)))
    rest = row - a * (fold * cap)
    b = jnp.floor((rest + 0.5) * (1.0 / cap))
    s = rest - b * cap
    source = (b * (fold * cap) + a * cap + s).astype(jnp.int32)
    lane = lax.broadcasted_iota(jnp.int32, (side, LANES), 1)
    parts = []
    for start in range(0, side, LANES):
        parts.append(jnp.where(source == lane + start, 1.0, 0.0).astype(BF16))
    return jnp.concatenate(parts, axis=1)


def slot_one_hot(routes_row, cap, slots):
    count = routes_row.shape[1]
    along = jnp.broadcast_to(routes_row.astype(F32), (count, count))
    down = along.T
    i = lax.broadcasted_iota(jnp.int32, (count, count), 0)
    j = lax.broadcasted_iota(jnp.int32, (count, count), 1)
    rank = jnp.sum(jnp.where((along == down) & (i < j), 1.0, 0.0), axis=0, keepdims=True)
    slot = (routes_row.astype(F32) * cap + rank).astype(jnp.int32)
    number = lax.broadcasted_iota(jnp.int32, (slots, count), 0)
    return jnp.where(number == slot, 1.0, 0.0).astype(BF16)


def pick_matrices(devices, cap):
    slots = devices * cap
    d = lax.broadcasted_iota(jnp.int32, (devices, slots), 0).astype(F32)
    slot = lax.broadcasted_iota(jnp.int32, (devices, slots), 1).astype(F32)
    owner = jnp.where(jnp.floor((slot + 0.5) * (1.0 / cap)) == d, 1.0, 0.0)
    slot = lax.broadcasted_iota(jnp.int32, (slots, LANES), 0).astype(F32)
    lane = lax.broadcasted_iota(jnp.int32, (slots, LANES), 1).astype(F32)
    rank = slot - jnp.floor((slot + 0.5) * (1.0 / cap)) * cap
    return owner, jnp.where(rank == lane, 1.0, 0.0)


def fold_group(swap, rows, fold):
    block, features = rows.shape
    chunk = features // fold
    stacked = jnp.concatenate([rows[:, c * chunk : (c + 1) * chunk] for c in range(fold)], axis=0)
    return dot(swap, stacked).astype(BF16).reshape(fold, block, chunk)


def unfold_group(swap, part):
    fold, block, chunk = part.shape
    rows = dot(swap, part.reshape(fold * block, chunk)).astype(BF16)
    return jnp.concatenate([rows[c * block : (c + 1) * block] for c in range(fold)], axis=1)


def layer_kernel(
    fold,
    cap,
    tokens_hbm,
    upstream_hbm,
    routes_hbm,
    shares_hbm,
    w_up_hbm,
    w_down_hbm,
    up_grad,
    down_grad,
    token_grad,
    gate_grad,
    tokens,
    upstream,
    routes,
    shares,
    w_up,
    w_down,
    w_up_t,
    send_tokens,
    send_scaled,
    got_tokens,
    got_scaled,
    send_back,
    got_back,
    send_sums,
    got_sums,
    token_rows,
    scaled_rows,
    hidden,
    slope,
    pre_grad,
    sums,
    send_sem,
    recv_sem,
    own_sem,
    load_sem,
):
    devices, block, chunk = send_tokens.shape
    count, features = tokens.shape
    slots = devices * cap
    groups = devices // fold
    side = groups // 2
    me = lax.axis_index("expert")
    place = lax.rem(me, fold)
    mine = lax.div(me, fold)
    lane = lax.rem(mine, side)
    near = mine - lane
    far = side - near
    channels = (
        (send_tokens, got_tokens),
        (send_scaled, got_scaled),
        (send_back, got_back),
        (send_sums, got_sums),
    )
    loads = [
        pltpu.make_async_copy(source, target, load_sem.at[number])
        for number, (source, target) in enumerate(
            (
                (routes_hbm, routes),
                (tokens_hbm, tokens),
                (shares_hbm, shares),
                (upstream_hbm, upstream),
                (w_up_hbm.at[0], w_up),
                (w_down_hbm.at[0], w_down),
            )
        )
    ]
    for load in loads:
        load.start()

    barrier = pltpu.get_barrier_semaphore()

    def greet(step, carry):
        pl.semaphore_signal(
            barrier, inc=1, device_id={"expert": lax.rem(me + step, devices)}, device_id_type=MESH
        )
        return carry

    lax.fori_loop(1, devices, greet, 0)

    def base_of(turn):
        return far + lax.div(turn, side) * (near - far)

    def shift_of(turn):
        return lax.rem(turn + lax.div(turn, side), side)

    def target_group(turn):
        return base_of(turn) + lax.rem(lane + shift_of(turn), side)

    def source_group(turn):
        return base_of(turn) + lax.rem(lane + side - shift_of(turn), side)

    def first_step(turn):
        return lax.div(turn, groups - 1)

    def push(k, turn, step):
        source, target = channels[k]
        peer = target_group(turn) * fold + lax.rem(place + step, fold)
        return pltpu.make_async_remote_copy(
            src_ref=source.at[peer],
            dst_ref=target.at[me],
            send_sem=send_sem.at[k, turn * fold + step],
            recv_sem=recv_sem.at[k, turn * fold + step],
            device_id={"expert": peer},
            device_id_type=MESH,
        )

    def arrival(k, turn, step):
        source, target = channels[k]
        came = source_group(turn) * fold + lax.rem(place + fold - step, fold)
        return pltpu.make_async_remote_copy(
            src_ref=source.at[came],
            dst_ref=target.at[came],
            send_sem=send_sem.at[k, turn * fold + step],
            recv_sem=recv_sem.at[k, turn * fold + step],
            device_id={"expert": came},
            device_id_type=MESH,
        )

    def send_turn(k, turn):
        def one(step, carry):
            push(k, turn, step).start()
            return carry

        lax.fori_loop(first_step(turn), fold, one, 0)

    def await_turn(k, turn):
        def one(step, carry):
            arrival(k, turn, step).wait_recv()
            return carry

        lax.fori_loop(first_step(turn), fold, one, 0)

    def every_turn(act, k):
        def one(turn, carry):
            act(k, turn)
            return carry

        lax.fori_loop(0, groups, one, 0)

    def settle(k, turn):
        def one(step, carry):
            push(k, turn, step).wait_send()
            return carry

        lax.fori_loop(first_step(turn), fold, one, 0)

    def own(k):
        source, target = channels[k]
        return pltpu.make_async_copy(source.at[me], target.at[me], own_sem.at[k])

    swap = swap_matrix(fold, cap)
    loads[0].wait()
    one_hot = slot_one_hot(routes[...], cap, slots)
    loads[1].wait()
    routed = dot(one_hot, tokens[...]).astype(BF16)
    for group in range(groups):
        rows = routed[group * block : (group + 1) * block]
        send_tokens[group * fold : (group + 1) * fold] = fold_group(swap, rows, fold)
    pl.semaphore_wait(barrier, devices - 1)
    every_turn(send_turn, 0)
    own(0).start()
    loads[2].wait()
    loads[3].wait()
    gate_row = shares[...].astype(F32) * (1.0 / GATE_DEN)
    gate = jnp.broadcast_to(gate_row, (count, count)).T
    scaled = jnp.concatenate(
        [
            (upstream[:, at : at + count].astype(F32) * gate).astype(BF16)
            for at in range(0, features, count)
        ],
        axis=1,
    )
    routed = dot(one_hot, scaled).astype(BF16)
    for group in range(groups):
        rows = routed[group * block : (group + 1) * block]
        send_scaled[group * fold : (group + 1) * fold] = fold_group(swap, rows, fold)
    every_turn(send_turn, 1)
    own(1).start()

    owner, rank = pick_matrices(devices, cap)
    loads[4].wait()
    loads[5].wait()
    w_up_t[...] = w_up[...].T
    every_turn(await_turn, 0)
    own(0).wait()
    for group in range(groups):
        token_rows[group * block : (group + 1) * block] = unfold_group(
            swap, got_tokens[group * fold : (group + 1) * fold]
        )
    pre = dot(token_rows[...], w_up[...])
    sigmoid = jax.nn.sigmoid(pre)
    hidden[...] = (pre * sigmoid).astype(BF16)
    slope[...] = sigmoid * (1.0 + pre * (1.0 - sigmoid))

    own(1).wait()

    def group_back(turn, carry):
        group = source_group(turn)
        devs = pl.ds(group * fold, fold)
        rows = pl.ds(pl.multiple_of(group * block, 16), block)
        await_turn(1, turn)
        part = unfold_group(swap, got_scaled[devs])
        scaled_rows[rows] = part
        cotangent = dot(part, w_down[...])
        grad = (cotangent * slope[rows]).astype(BF16)
        pre_grad[rows] = grad
        send_back[devs] = fold_group(swap, dot(grad, w_up_t[...]).astype(BF16), fold)
        back_turn(turn)
        total = jnp.sum(hidden[rows].astype(F32) * cotangent, axis=1, keepdims=True)
        sums[rows] = jnp.broadcast_to(total.astype(BF16).astype(F32), (block, LANES))
        return carry

    def back_turn(turn):
        def one(step, carry):
            peer = source_group(turn) * fold + lax.rem(place + fold - step, fold)
            pltpu.make_async_remote_copy(
                src_ref=send_back.at[peer],
                dst_ref=got_back.at[me],
                send_sem=send_sem.at[2, turn * fold + step],
                recv_sem=recv_sem.at[2, turn * fold + step],
                device_id={"expert": peer},
                device_id_type=MESH,
            ).start()
            return carry

        lax.fori_loop(first_step(turn), fold, one, 0)

    lax.fori_loop(0, groups, group_back, 0)
    own(2).start()
    send_sums[...] = dot(owner.astype(BF16), (sums[...] * rank).astype(BF16)).reshape(
        devices, 1, LANES
    )
    every_turn(send_turn, 3)
    own(3).start()

    tile = 256

    def weights(i, carry):
        at = pl.ds(pl.multiple_of(i * tile, tile), tile)
        up_grad[at] = dot(token_rows[:, at], pre_grad[...], ((0,), (0,))).astype(BF16)
        down_grad[at] = dot(scaled_rows[:, at], hidden[...], ((0,), (0,))).astype(BF16)
        return carry

    lax.fori_loop(0, features // tile, weights, 0)

    every_turn(await_turn, 3)
    own(3).wait()
    picked = dot(owner.astype(BF16), got_sums[...].reshape(devices, LANES).astype(BF16), ((0,), (0,)))
    picked = jnp.sum(picked * rank, axis=1, keepdims=True)
    per_token = jnp.sum(picked * one_hot.astype(F32), axis=0, keepdims=True)
    gate_grad[...] = (per_token / gate_row).astype(BF16)
    for k in (0, 1, 2, 3):
        every_turn(settle, k)

    def await_back(turn, carry):
        def one(step, inner):
            peer = target_group(turn) * fold + lax.rem(place + step, fold)
            pltpu.make_async_remote_copy(
                src_ref=send_back.at[peer],
                dst_ref=got_back.at[peer],
                send_sem=send_sem.at[2, turn * fold + step],
                recv_sem=recv_sem.at[2, turn * fold + step],
                device_id={"expert": peer},
                device_id_type=MESH,
            ).wait_recv()
            return inner

        lax.fori_loop(first_step(turn), fold, one, 0)
        return carry

    lax.fori_loop(0, groups, await_back, 0)
    own(2).wait()
    for group in range(groups):
        token_rows[group * block : (group + 1) * block] = unfold_group(
            swap, got_back[group * fold : (group + 1) * fold]
        )
    token_grad[...] = dot(one_hot, token_rows[...], ((0,), (0,))).astype(BF16)


def per_device(tokens, upstream, w_up, w_down, routes, gate_share):
    count, features = tokens.shape
    units = w_up.shape[2]
    devices = lax.axis_size("expert")
    groups = lax.axis_size("dp")
    cap = (3 * count + 2 * devices - 1) // (2 * devices)
    fold = 16 // math.gcd(16, cap)
    block, chunk = fold * cap, features // fold
    slots = devices * cap
    routes_row, shares_row = routes.reshape(1, count), gate_share.reshape(1, count)
    whole = pl.BlockSpec(memory_space=pltpu.VMEM)
    buffer = pltpu.VMEM((devices, block, chunk), BF16)
    sums = pltpu.VMEM((devices, 1, LANES), F32)
    up_grad, down_grad, token_grad, gate_grad = pl.pallas_call(
        functools.partial(layer_kernel, fold, cap),
        in_specs=[pl.BlockSpec(memory_space=pltpu.HBM)] * 6,
        out_specs=[whole] * 4,
        out_shape=[
            jax.ShapeDtypeStruct((features, units), BF16),
            jax.ShapeDtypeStruct((features, units), BF16),
            jax.ShapeDtypeStruct((count, features), BF16),
            jax.ShapeDtypeStruct((1, count), BF16),
        ],
        scratch_shapes=[
            pltpu.VMEM((count, features), BF16),
            pltpu.VMEM((count, features), BF16),
            pltpu.VMEM((1, count), jnp.int32),
            pltpu.VMEM((1, count), jnp.int32),
            pltpu.VMEM((features, units), BF16),
            pltpu.VMEM((features, units), BF16),
            pltpu.VMEM((units, features), BF16),
            *([buffer] * 6),
            sums,
            sums,
            pltpu.VMEM((slots, features), BF16),
            pltpu.VMEM((slots, features), BF16),
            pltpu.VMEM((slots, units), BF16),
            pltpu.VMEM((slots, units), F32),
            pltpu.VMEM((slots, units), BF16),
            pltpu.VMEM((slots, LANES), F32),
            pltpu.SemaphoreType.DMA((4, devices)),
            pltpu.SemaphoreType.DMA((4, devices)),
            pltpu.SemaphoreType.DMA((4,)),
            pltpu.SemaphoreType.DMA((6,)),
        ],
        compiler_params=pltpu.CompilerParams(
            collective_id=1, has_side_effects=True, vmem_limit_bytes=48 << 20
        ),
    )(tokens, upstream, routes_row, shares_row, w_up, w_down)
    up_grad, down_grad = up_grad[None], down_grad[None]
    if groups > 1:
        up_grad, down_grad = (
            lax.psum_scatter(g, "dp", scatter_dimension=1, tiled=True)
            for g in (up_grad, down_grad)
        )
    return token_grad, gate_grad.reshape(count, 1), up_grad.astype(F32), down_grad.astype(F32)


def solution(mesh):
    rows, experts = P(("dp", "expert"), None), P("expert", None, None)
    return jax.shard_map(
        per_device,
        mesh=mesh,
        in_specs=(rows, rows, experts, experts, rows, rows),
        out_specs=(rows, rows, P("expert", "dp", None), P("expert", "dp", None)),
        check_vma=False,
    )
```

time: 80.5 us -> 80.2 us (level)
  Pallas kernels: 75 us -> 67 us
  other arithmetic: 0 us -> 7.58 us
    pallas_call x2 -> x1, Pallas kernels: 75 us -> 67 us  [per_device(): pl.pallas_call(functools.partial(layer_kernel, fold, cap), in_specs=[pl.B...]
    convert_element_type x0 -> x1, other arithmetic: none -> 7.58 us  [per_device(): down_grad.astype(F32)]
where the time goes in v3:
time: 80.2 us; the launch traced here: 80 us
  Pallas kernels  67 us (84%)
  other arithmetic  7.58 us (9%)
  local copies, waits for them, and re-layouts  4.69 us (6%)
    pallas_call x1, Pallas kernels, per_device(): pl.pallas_call(functools.partial(layer_kernel, fold, cap), in_specs=[pl.B...  67 us
    convert_element_type x1, other arithmetic, per_device(): down_grad.astype(F32)  7.58 us
    unnamed x10, local copies, waits for them, and re-layouts  4.69 us

profile of v3, /device:TPU:0, one launch (start us, length us, event | category | flops | bytes accessed | tf_op | source)
XLA Modules:
  0.0 80.0 jit_solution(2808694981333807537)
XLA Ops:
  0.6 0.0 copy-start
  0.6 1.0 %copy-done = bf16[128,2048]{1,0:T(8,128)(2,1)S(1)} copy-done((bf16[128,2048]{1,0:T(8,128)(2,1)S(1)}, bf16[128,2048]{1,0:T(8,128)(2,1)}, u32[]{:S(2)}) %copy-start) | copy-done | bytes 524312
  1.7 0.0 copy-start.1
  1.7 1.0 %copy-done.1 = bf16[128,2048]{1,0:T(8,128)(2,1)S(1)} copy-done((bf16[128,2048]{1,0:T(8,128)(2,1)S(1)}, bf16[128,2048]{1,0:T(8,128)(2,1)}, u32[]{:S(2)}) %copy-start.1) | copy-done | bytes 524312
  2.7 0.0 copy-start.2
  2.7 0.7 copy-done.2
  3.4 0.0 copy-start.3
  3.4 0.7 copy-done.3
  4.0 67.0 %shard_map.93 = (bf16[2048,768]{1,0:T(8,128)(2,1)S(1)}, bf16[2048,768]{1,0:T(8,128)(2,1)}, bf16[128,2048]{1,0:T(8,128)(2,1)S(1)}, bf16[1,128]{1,0:T(2,128)(2,1)S(1)}) custom-call(bf16[128,2048]{1,0:T(8,128)(2,1)S(1)} %copy-done, bf16[128,2048]{1,0:T(8,128)(2,1)S(1)} %copy-done.1, s32[1,128]{1,0:T(1,128)S(1)} %bitcast.9, s32[1,128]{1,0:T(1,128)S(1)} %bitcast.10, ...), custom_call_target="tpu_custom_call" | custom-call | tf_op jit(solution)/shard_map/pallas_call | solution.py:368
  71.1 7.6 %bitcast_convert_fusion = (f32[1,2048,768]{2,1,0:T(8,128)}, f32[1,2048,768]{2,1,0:T(8,128)}) fusion(bf16[2048,768]{1,0:T(8,128)(2,1)} %get-tuple-element.11, bf16[2048,768]{1,0:T(8,128)(2,1)S(1)} %get-tuple-element.10), kind=kLoop, calls=%fused_computation | loop fusion | flops 3145728 | bytes 18874368 | tf_op jit(solution)/shard_map/convert_element_type | solution.py:410
  78.7 0.8 copy.12
  79.5 0.5 copy.13
Async XLA Ops:
  0.6 1.0 %copy-start = (bf16[128,2048]{1,0:T(8,128)(2,1)S(1)}, bf16[128,2048]{1,0:T(8,128)(2,1)}, u32[]{:S(2)}) copy-start(bf16[128,2048]{1,0:T(8,128)(2,1)} %tokens_hbm.1) | copy-start | bytes 1572868
  1.7 1.0 %copy-start.1 = (bf16[128,2048]{1,0:T(8,128)(2,1)S(1)}, bf16[128,2048]{1,0:T(8,128)(2,1)}, u32[]{:S(2)}) copy-start(bf16[128,2048]{1,0:T(8,128)(2,1)} %upstream_hbm.1) | copy-start | bytes 1572868
  2.7 0.7 copy-start.2
  3.4 0.7 copy-start.3

commit v4 on v3

--- a/solution.py
+++ b/solution.py
@@ -79,8 +79,10 @@
     shares_hbm,
     w_up_hbm,
     w_down_hbm,
-    up_grad,
-    down_grad,
+    token_rows,
+    scaled_rows,
+    hidden,
+    pre_grad,
     token_grad,
     gate_grad,
     tokens,
@@ -98,11 +100,8 @@
     got_back,
     send_sums,
     got_sums,
-    token_rows,
-    scaled_rows,
-    hidden,
+    back_rows,
     slope,
-    pre_grad,
     sums,
     send_sem,
     recv_sem,
@@ -308,16 +307,6 @@
     every_turn(send_turn, 3)
     own(3).start()
 
-    tile = 256
-
-    def weights(i, carry):
-        at = pl.ds(pl.multiple_of(i * tile, tile), tile)
-        up_grad[at] = dot(token_rows[:, at], pre_grad[...], ((0,), (0,))).astype(BF16)
-        down_grad[at] = dot(scaled_rows[:, at], hidden[...], ((0,), (0,))).astype(BF16)
-        return carry
-
-    lax.fori_loop(0, features // tile, weights, 0)
-
     every_turn(await_turn, 3)
     own(3).wait()
     picked = dot(owner.astype(BF16), got_sums[...].reshape(devices, LANES).astype(BF16), ((0,), (0,)))
@@ -346,10 +335,17 @@
     lax.fori_loop(0, groups, await_back, 0)
     own(2).wait()
     for group in range(groups):
-        token_rows[group * block : (group + 1) * block] = unfold_group(
+        back_rows[group * block : (group + 1) * block] = unfold_group(
             swap, got_back[group * fold : (group + 1) * fold]
         )
-    token_grad[...] = dot(one_hot, token_rows[...], ((0,), (0,))).astype(BF16)
+    token_grad[...] = dot(one_hot, back_rows[...], ((0,), (0,))).astype(BF16)
+
+
+def weight_kernel(tokens, scaled, hidden, pre_grad, up_grad, down_grad):
+    up = dot(tokens[...], pre_grad[...], ((0,), (0,))).astype(BF16)
+    down = dot(scaled[...], hidden[...], ((0,), (0,))).astype(BF16)
+    up_grad[...] = up.astype(up_grad.dtype)[None]
+    down_grad[...] = down.astype(down_grad.dtype)[None]
 
 
 def per_device(tokens, upstream, w_up, w_down, routes, gate_share):
@@ -365,13 +361,15 @@
     whole = pl.BlockSpec(memory_space=pltpu.VMEM)
     buffer = pltpu.VMEM((devices, block, chunk), BF16)
     sums = pltpu.VMEM((devices, 1, LANES), F32)
-    up_grad, down_grad, token_grad, gate_grad = pl.pallas_call(
+    got_tokens, got_scaled, hidden, pre_grad, token_grad, gate_grad = pl.pallas_call(
         functools.partial(layer_kernel, fold, cap),
         in_specs=[pl.BlockSpec(memory_space=pltpu.HBM)] * 6,
-        out_specs=[whole] * 4,
+        out_specs=[whole] * 6,
         out_shape=[
-            jax.ShapeDtypeStruct((features, units), BF16),
-            jax.ShapeDtypeStruct((features, units), BF16),
+            jax.ShapeDtypeStruct((slots, features), BF16),
+            jax.ShapeDtypeStruct((slots, features), BF16),
+            jax.ShapeDtypeStruct((slots, units), BF16),
+            jax.ShapeDtypeStruct((slots, units), BF16),
             jax.ShapeDtypeStruct((count, features), BF16),
             jax.ShapeDtypeStruct((1, count), BF16),
         ],
@@ -387,10 +385,7 @@
             sums,
             sums,
             pltpu.VMEM((slots, features), BF16),
-            pltpu.VMEM((slots, features), BF16),
-            pltpu.VMEM((slots, units), BF16),
             pltpu.VMEM((slots, units), F32),
-            pltpu.VMEM((slots, units), BF16),
             pltpu.VMEM((slots, LANES), F32),
             pltpu.SemaphoreType.DMA((4, devices)),
             pltpu.SemaphoreType.DMA((4, devices)),
@@ -398,10 +393,24 @@
             pltpu.SemaphoreType.DMA((6,)),
         ],
         compiler_params=pltpu.CompilerParams(
-            collective_id=1, has_side_effects=True, vmem_limit_bytes=48 << 20
+            collective_id=1, has_side_effects=True, vmem_limit_bytes=127 << 19
         ),
     )(tokens, upstream, routes_row, shares_row, w_up, w_down)
-    up_grad, down_grad = up_grad[None], down_grad[None]
+    tile = 256
+    kind = F32 if groups == 1 else BF16
+    up_grad, down_grad = pl.pallas_call(
+        weight_kernel,
+        grid=(features // tile,),
+        in_specs=[
+            pl.BlockSpec((slots, tile), lambda i: (0, i)),
+            pl.BlockSpec((slots, tile), lambda i: (0, i)),
+            pl.BlockSpec((slots, units), lambda i: (0, 0)),
+            pl.BlockSpec((slots, units), lambda i: (0, 0)),
+        ],
+        out_specs=[pl.BlockSpec((1, tile, units), lambda i: (0, i, 0))] * 2,
+        out_shape=[jax.ShapeDtypeStruct((1, features, units), kind)] * 2,
+        compiler_params=pltpu.CompilerParams(vmem_limit_bytes=127 << 19),
+    )(got_tokens, got_scaled, hidden, pre_grad)
     if groups > 1:
         up_grad, down_grad = (
             lax.psum_scatter(g, "dp", scatter_dimension=1, tiled=True)

time: 80.2 us -> 79.6 us (level)
  Pallas kernels: 67 us -> 75.4 us
  other arithmetic: 7.58 us -> 0 us
  local copies, waits for them, and re-layouts: 4.69 us -> 3.06 us
    pallas_call x0 -> x1, Pallas kernels: none -> 8.52 us  [per_device(): pl.pallas_call(weight_kernel, grid=(features // tile,), in_specs=[pl.Bloc...]
    convert_element_type x1 -> x0, other arithmetic: 7.58 us -> none  [per_device(): down_grad.astype(F32)]
    unnamed x10 -> x2, local copies, waits for them, and re-layouts: 4.69 us -> 3.06 us
where the time goes in v4:
time: 79.6 us; the launch traced here: 79.1 us
  Pallas kernels  75.4 us (95%)
  local copies, waits for them, and re-layouts  3.06 us (4%)
    pallas_call x1, Pallas kernels, per_device(): pl.pallas_call(functools.partial(layer_kernel, fold, cap), in_specs=[pl.B...  66.9 us
    pallas_call x1, Pallas kernels, per_device(): pl.pallas_call(weight_kernel, grid=(features // tile,), in_specs=[pl.Bloc...  8.52 us
    unnamed x2, local copies, waits for them, and re-layouts  3.06 us

profile of v4, /device:TPU:0, one launch (start us, length us, event | category | flops | bytes accessed | tf_op | source)
XLA Modules:
  0.0 79.1 jit_solution(658993099759568940)
XLA Ops:
  0.6 66.9 %shard_map.93 = (bf16[192,2048]{1,0:T(8,128)(2,1)}, bf16[192,2048]{1,0:T(8,128)(2,1)}, bf16[192,768]{1,0:T(8,128)(2,1)}, bf16[192,768]{1,0:T(8,128)(2,1)}, bf16[...) custom-call(bf16[128,2048]{1,0:T(8,128)(2,1)} %tokens_hbm.1, bf16[128,2048]{1,0:T(8,128)(2,1)} %upstream_hbm.1, ...), custom_call_target="tpu_custom_call" | custom-call | tf_op jit(solution)/shard_map/pallas_call | solution.py:364
  67.5 8.5 %shard_map.94 = (f32[1,2048,768]{2,1,0:T(8,128)}, f32[1,2048,768]{2,1,0:T(8,128)}) custom-call(bf16[192,2048]{1,0:T(8,128)(2,1)} %get-tuple-element.14.tokens, bf16[192,2048]{1,0:T(8,128)(2,1)} %get-tuple-element.15.scaled, bf16[192,768]{1,0:T(8,128)(2,1)} %get-tuple-element.16.hidden, bf16[192,768]{1,0:T(8,128)(2,1)} %get-tuple-element.17.pre_grad), custom_call_target="tpu_custom_call" | custom-call | tf_op jit(solution)/shard_map/pallas_call | solution.py:401
  76.1 1.9 %copy.12 = bf16[128,2048]{1,0:T(8,128)(2,1)} copy(bf16[128,2048]{1,0:T(8,128)(2,1)} %get-tuple-element.24) | data formatting | bytes 1048576
  78.0 1.2 %copy.13 = bf16[128,1]{0,1:T(2,128)(2,1)} copy(bf16[128,1]{0,1:T(2,128)(2,1)} %bitcast.5) | data formatting | bytes 512
